TPU v7x, 32 devices: a whole 2x2x4 slice. The times are simulated.
32 devices in a mesh: sta: 16 (over z, y, core), day: 2 (over x).
Axes of the slice: x: 2, y: 2, z: 4, core: 2. Of those that a mesh axis runs over, the one named last changes fastest.
Arguments:
- spectra: bfloat16 [2, 12, 2, 768, 640], P('day', None, None, 'sta'), as said below
- window_valid: int32 [2, 12], replicated, may hold values 0 or 1
- owner_order: int32 [4], replicated, may hold values from 0 to 15
Outputs:
- correlations: bfloat16 [4, 48, 768, 256], P(None, 'day', 'sta')
Inputs may be any that keep to these rules, and one draw needn't show every extreme that they name: `spectra`: finite values.
All inputs are finite; a program needn't handle non-finite values.
Results may differ from a plain program's by a relative error of at most 0.0073.
Values may be sent and summed in bfloat16 or wider, within the bound.
A program may use at most 192 MiB of HBM per device.

v0:
```python
import math

import jax
import jax.numpy as jnp
from jax import lax
from jax.sharding import PartitionSpec as P

STEPS = 4
LAGS = 256
NFFT = 2400
FIRST_BIN = 60


def broadcast(value, axis, root):
    mine = lax.axis_index(axis) == root
    return lax.psum(jnp.where(mine, value, jnp.zeros_like(value)), axis)


def whiten(spectra):
    values = spectra.astype(jnp.float32)
    energy = jnp.mean(values * values, axis=(2, 4), keepdims=True)
    return (values / jnp.sqrt(energy + 1e-06)).astype(jnp.bfloat16)


def lag_table(bins, lag_count):
    freq_index = FIRST_BIN + lax.iota(jnp.int32, bins)
    lag_index = lax.iota(jnp.int32, lag_count) - lag_count // 2
    phase = freq_index[:, None] * lag_index[None, :] % NFFT
    angle = phase.astype(jnp.float32) * (2.0 * math.pi / NFFT)
    return jnp.stack([jnp.cos(angle), -jnp.sin(angle)]).astype(jnp.bfloat16)


def day_correlation(owner, local, day_valid, lag_grid, stack_scale):
    masked = owner * day_valid.astype(jnp.bfloat16)[:, None, None, None]
    turned = jnp.stack([local, jnp.concatenate([-local[:, 1:2], local[:, 0:1]], axis=1)], axis=2)
    cross = jnp.einsum("wcaf,wckbf->fakb", masked, turned, preferred_element_type=jnp.float32)
    cross = (cross * stack_scale).astype(jnp.bfloat16)
    lag_sums = jnp.einsum("fakb,kft->abt", cross, lag_grid, preferred_element_type=jnp.float32)
    return lag_sums * (1.0 / math.sqrt(cross.shape[0]))


def body(spectra, window_valid, owner_order):
    day_index = lax.axis_index("day")
    whitened = whiten(spectra)[0]
    lag_grid = lag_table(whitened.shape[3], LAGS)
    stack_scale = 1.0 / math.sqrt(lax.axis_size("day") * whitened.shape[0])
    own_valid = lax.dynamic_index_in_dim(window_valid, day_index, 0, keepdims=False)
    results = []
    for step_index in range(STEPS):
        owner = broadcast(whitened, "sta", owner_order[step_index])
        lag_sums = day_correlation(owner, whitened, own_valid, lag_grid, stack_scale)
        share = lax.psum_scatter(
            lag_sums.astype(jnp.bfloat16), "day", scatter_dimension=0, tiled=True
        )
        results.append(share)
    return jnp.stack(results)


def solution(mesh):
    return jax.shard_map(
        body,
        mesh=mesh,
        in_specs=(P("day", None, None, "sta", None), P(), P()),
        out_specs=P(None, "day", "sta", None),
        check_vma=False,
    )
```

profile of v0, /device:TPU:0, one launch (start us, length us, event | category | flops | bytes accessed | tf_op | source)
XLA Modules:
  0.0 420.9 jit_solution(7589611989793982384)
XLA Ops:
  6.5 1.5 fusion.41
  10.5 1.7 fusion.16
  12.3 4.4 %broadcast_select_fusion.3 = (bf16[12,2,48,640]{3,2,1,0:T(8,128)(2,1)}, bf16[12,2,48,640]{3,2,1,0:T(8,128)(2,1)}, bf16[12,2,48,640]{3,2,1,0:T(8,128)(2,1)}, bf16[12,2,48,640]{3,2,1,0:T(8,128)(2,1)}) fusion(pred[]{:T(512)S(6)} %eq.14, f32[12,48]{1,0:T(8,128)S(1)} %add_sqrt_fusion, bf16[1,12,2,48,640]{4,3,2,1,0:T(8,128)(2,1)} %param.3, pred[]{:T(512)S(6)} %eq.17, ...), kind=kLoop, calls=%fused_computation.38 | loop fusion | flops 5160960 | bytes 7375108 | tf_op jit(solution)/shard_map/jit(_where)/select_n | solution.py:16
  16.8 1.3 copy-done
  18.1 0.4 fusion.39
  18.7 0.2 maximum_bitcast_fusion
  18.8 0.3 pad_maximum_fusion
  19.1 15.1 %copy.5 = bf16[12,2,2,48,640]{3,0,1,2,4:T(8,128)(2,1)} copy(bf16[12,2,2,48,640]{4,3,1,0,2:T(8,128)(2,1)S(1)} %pad_maximum_fusion) | data formatting | bytes 5898240 | tf_op jit(solution)/shard_map/stack | solution.py:35
  34.3 3.1 cosine_convert_fusion
  37.5 116.6 %all-reduce.3.cloned.1.call-done = (bf16[12,2,48,640]{3,2,1,0:T(8,128)(2,1)}, bf16[12,2,48,640]{3,2,1,0:T(8,128)(2,1)}, bf16[12,2,48,640]{3,2,1,0:T(8,128)(2,1)}, bf16[12,2,48,640]{3,2,1,0:T(8,128)(2,1)}) async-done(((bf16[12,2,48,640]{3,2,1,0:T(8,128)(2,1)}, bf16[12,2,48,640]{3,2,1,0:T(8,128)(2,1)}, bf16[12,2,48,640]{3,2,1,0:T(8,128)(2,1)}, bf16[12,2,48,640]{3,2,1,0:T(8,128)(2,1)}), ...) | async-done | bytes 5898256 | tf_op jit(solution)/shard_map/psum | solution.py:16
  154.0 5.1 %multiply_bitcast_fusion.3 = (bf16[12,2,48,640,1]{3,2,1,0,4:T(8,128)(2,1)}, bf16[12,2,48,640,1]{3,2,1,0,4:T(8,128)(2,1)}, bf16[12,2,48,640,1]{3,2,1,0,4:T(8,128)(2,1)}, bf16[12,2,48,640,1]{3,2,1,0,4:T(8,128)(2,1)S(1)}) fusion(bf16[12,2,48,640]{3,2,1,0:T(8,128)(2,1)} %get-tuple-element.8, bf16[12]{0:T(256)(128)(2,1)S(1)} %convert_bitcast_fusion, ...), kind=kLoop, calls=%fused_computation.34 | loop fusion | flops 2949120 | bytes 11796504 | tf_op jit(solution)/shard_map/mul | solution.py:34
  159.1 8.7 %copy.4 = bf16[12,2,48,640,1]{2,0,1,4,3:T(8,128)(2,1)} copy(bf16[12,2,48,640,1]{3,2,1,0,4:T(8,128)(2,1)} %get-tuple-element.19) | data formatting | bytes 2949120 | tf_op jit(solution)/shard_map/mul | solution.py:34
  167.8 16.2 %fusion.42 = f32[640,48,2,48,1]{3,1,4,2,0:T(8,128)} fusion(bf16[12,2,48,640,1]{2,0,1,4,3:T(8,128)(2,1)} %copy.4, bf16[12,2,2,48,640]{3,0,1,2,4:T(8,128)(2,1)} %copy.5), kind=kOutput, calls=%fused_computation.61 | convolution fusion | flops 141557760 | bytes 16220160 | tf_op jit(solution)/shard_map/wcaf,wckbf->fakb/dot_general | solution.py:36
  184.1 25.2 %copy.6 = f32[640,48,2,48,1]{0,3,2,1,4:T(8,128)} copy(f32[640,48,2,48,1]{3,1,4,2,0:T(8,128)} %fusion.42) | data formatting | bytes 23592960 | tf_op jit(solution)/shard_map/wcaf,wckbf->fakb/dot_general | solution.py:36
  209.3 7.1 %fusion.21 = bf16[48,48,256]{2,1,0:T(8,128)(2,1)} fusion(f32[640,48,2,48,1]{0,3,2,1,4:T(8,128)} %copy.6, bf16[1,640,256]{2,1,0:T(8,128)(2,1)S(1)} %get-tuple-element.18, bf16[1,640,256]{2,1,0:T(8,128)(2,1)S(1)} %get-tuple-element.17), kind=kOutput, calls=%fused_computation.29 | convolution fusion | flops 1517355008 | bytes 13631488 | tf_op jit(solution)/shard_map/fakb,kft->abt/dot_general | solution.py:38
  216.4 0.2 reduce-scatter.7.cloned.1.call-start
  216.6 8.7 %copy.8 = bf16[12,2,48,640,1]{2,0,1,4,3:T(8,128)(2,1)} copy(bf16[12,2,48,640,1]{3,2,1,0,4:T(8,128)(2,1)} %get-tuple-element.20) | data formatting | bytes 2949120 | tf_op jit(solution)/shard_map/mul | solution.py:34
  225.3 16.4 %fusion.43 = f32[640,48,2,48,1]{3,1,4,2,0:T(8,128)} fusion(bf16[12,2,48,640,1]{2,0,1,4,3:T(8,128)(2,1)} %copy.8, bf16[12,2,2,48,640]{3,0,1,2,4:T(8,128)(2,1)} %copy.5), kind=kOutput, calls=%fused_computation.62 | convolution fusion | flops 141557760 | bytes 16220160 | tf_op jit(solution)/shard_map/wcaf,wckbf->fakb/dot_general | solution.py:36
  241.7 25.2 %copy.9 = f32[640,48,2,48,1]{0,3,2,1,4:T(8,128)} copy(f32[640,48,2,48,1]{3,1,4,2,0:T(8,128)} %fusion.43) | data formatting | bytes 23592960 | tf_op jit(solution)/shard_map/wcaf,wckbf->fakb/dot_general | solution.py:36
  266.9 8.7 %copy.11 = bf16[12,2,48,640,1]{2,0,1,4,3:T(8,128)(2,1)} copy(bf16[12,2,48,640,1]{3,2,1,0,4:T(8,128)(2,1)} %get-tuple-element.21) | data formatting | bytes 2949120 | tf_op jit(solution)/shard_map/mul | solution.py:34
  275.6 7.1 %fusion.20 = bf16[48,48,256]{2,1,0:T(8,128)(2,1)} fusion(f32[640,48,2,48,1]{0,3,2,1,4:T(8,128)} %copy.9, bf16[1,640,256]{2,1,0:T(8,128)(2,1)S(1)} %get-tuple-element.18, bf16[1,640,256]{2,1,0:T(8,128)(2,1)S(1)} %get-tuple-element.17), kind=kOutput, calls=%fused_computation.27 | convolution fusion | flops 1517355008 | bytes 13631488 | tf_op jit(solution)/shard_map/fakb,kft->abt/dot_general | solution.py:38
  282.8 0.3 reduce-scatter.9.cloned.1.call-start
  283.1 16.5 %fusion.44 = f32[640,48,2,48,1]{3,1,4,2,0:T(8,128)} fusion(bf16[12,2,48,640,1]{2,0,1,4,3:T(8,128)(2,1)} %copy.11, bf16[12,2,2,48,640]{3,0,1,2,4:T(8,128)(2,1)} %copy.5), kind=kOutput, calls=%fused_computation.63 | convolution fusion | flops 141557760 | bytes 16220160 | tf_op jit(solution)/shard_map/wcaf,wckbf->fakb/dot_general | solution.py:36
  299.5 25.2 %copy.12 = f32[640,48,2,48,1]{0,3,2,1,4:T(8,128)} copy(f32[640,48,2,48,1]{3,1,4,2,0:T(8,128)} %fusion.44) | data formatting | bytes 23592960 | tf_op jit(solution)/shard_map/wcaf,wckbf->fakb/dot_general | solution.py:36
  324.8 8.1 %copy.14 = bf16[12,2,48,640,1]{2,0,1,4,3:T(8,128)(2,1)} copy(bf16[12,2,48,640,1]{3,2,1,0,4:T(8,128)(2,1)S(1)} %get-tuple-element.22) | data formatting | bytes 2949120 | tf_op jit(solution)/shard_map/mul | solution.py:34
  332.8 7.1 %fusion.19 = bf16[48,48,256]{2,1,0:T(8,128)(2,1)} fusion(f32[640,48,2,48,1]{0,3,2,1,4:T(8,128)} %copy.12, bf16[1,640,256]{2,1,0:T(8,128)(2,1)S(1)} %get-tuple-element.18, bf16[1,640,256]{2,1,0:T(8,128)(2,1)S(1)} %get-tuple-element.17), kind=kOutput, calls=%fused_computation.25 | convolution fusion | flops 1517355008 | bytes 13631488 | tf_op jit(solution)/shard_map/fakb,kft->abt/dot_general | solution.py:38
  339.9 0.3 reduce-scatter.11.cloned.1.call-start
  340.2 16.5 %fusion.45 = f32[640,48,2,48,1]{3,1,4,2,0:T(8,128)} fusion(bf16[12,2,48,640,1]{2,0,1,4,3:T(8,128)(2,1)} %copy.14, bf16[12,2,2,48,640]{3,0,1,2,4:T(8,128)(2,1)} %copy.5), kind=kOutput, calls=%fused_computation.64 | convolution fusion | flops 141557760 | bytes 16220160 | tf_op jit(solution)/shard_map/wcaf,wckbf->fakb/dot_general | solution.py:36
  356.7 25.2 %copy.15 = f32[640,48,2,48,1]{0,3,2,1,4:T(8,128)} copy(f32[640,48,2,48,1]{3,1,4,2,0:T(8,128)} %fusion.45) | data formatting | bytes 23592960 | tf_op jit(solution)/shard_map/wcaf,wckbf->fakb/dot_general | solution.py:36
  381.9 7.1 %fusion.18 = bf16[48,48,256]{2,1,0:T(8,128)(2,1)} fusion(f32[640,48,2,48,1]{0,3,2,1,4:T(8,128)} %copy.15, bf16[1,640,256]{2,1,0:T(8,128)(2,1)S(1)} %get-tuple-element.18, bf16[1,640,256]{2,1,0:T(8,128)(2,1)S(1)} %get-tuple-element.17), kind=kOutput, calls=%fused_computation.23 | convolution fusion | flops 1517355008 | bytes 13631488 | tf_op jit(solution)/shard_map/fakb,kft->abt/dot_general | solution.py:38
  389.1 22.0 %reduce-scatter.11.cloned.1.call-done = bf16[24,48,256]{2,1,0:T(8,128)(2,1)} async-done(((bf16[48,48,256]{2,1,0:T(8,128)(2,1)}), bf16[24,48,256]{2,1,0:T(8,128)(2,1)}) %reduce-scatter.11.cloned.1.call-update) | async-done | bytes 589840 | tf_op jit(solution)/shard_map/reduce_scatter | solution.py:52
  411.1 3.3 pad_maximum_fusion.1
  (18 shorter events, 0.3 us)
Async XLA Ops:
  6.5 147.5 %all-reduce.3.cloned.1.call-start = ((), (), s32[]{:S(2)}) async-start(), calls=%async_computation.8 | async-start | bytes 11796480 | tf_op jit(solution)/shard_map/psum | solution.py:16
  16.7 1.4 copy-start
  16.7 372.3 %reduce-scatter.5.cloned.1.call-start = ((), (), s32[]{:S(2)}) async-start(), calls=%async_computation.4 | async-start | bytes 1769472 | tf_op jit(solution)/shard_map/reduce_scatter | solution.py:52
  19.1 15.2 %copy-start.1 = (s32[2,12]{1,0:T(2,128)S(1)}, s32[2,12]{1,0:T(2,128)}, u32[]{:S(2)}) copy-start(s32[2,12]{1,0:T(2,128)} %param.4) | copy-start | bytes 292
  216.4 172.6 %reduce-scatter.7.cloned.1.call-start = ((), (), s32[]{:S(2)}) async-start(), calls=%async_computation.5 | async-start | bytes 1769472 | tf_op jit(solution)/shard_map/reduce_scatter | solution.py:52
  282.8 106.3 %reduce-scatter.9.cloned.1.call-start = ((), (), s32[]{:S(2)}) async-start(), calls=%async_computation.6 | async-start | bytes 1769472 | tf_op jit(solution)/shard_map/reduce_scatter | solution.py:52
  339.9 71.2 %reduce-scatter.11.cloned.1.call-start = ((), (), s32[]{:S(2)}) async-start(), calls=%async_computation.7 | async-start | bytes 1769472 | tf_op jit(solution)/shard_map/reduce_scatter | solution.py:52
Sparse Core Ops, SparseCore 0:
  16.9 137.1 all-reduce.2
  216.5 21.7 reduce-scatter.4
  282.9 21.7 reduce-scatter.6
  340.0 21.8 reduce-scatter.8
  389.1 21.9 reduce-scatter.10
where the time goes:
time: 423 us; the launch traced here: 421 us
  local copies, waits for them, and re-layouts  153 us (36%)
  waiting for transfers between devices  139 us (33%)
  matrix products  93.9 us (22%)
  other arithmetic  18.7 us (4%)
  between operations  15.8 us (4%)
    psum x1, waiting for transfers between devices, broadcast(): return lax.psum(jnp.where(mine, value, jnp.zeros_like(value)), axis)  117 us
    dot_general x4, local copies, waits for them, and re-layouts, day_correlation(): jnp.einsum('wcaf,wckbf->fakb', masked, turned, preferred_element_type=jnp...  101 us
    dot_general x4, matrix products, day_correlation(): jnp.einsum('wcaf,wckbf->fakb', masked, turned, preferred_element_type=jnp...  65.6 us
    mul x4, local copies, waits for them, and re-layouts, day_correlation(): masked = owner * day_valid.astype(jnp.bfloat16)[:, None, None, None]  34.2 us
    dot_general x4, matrix products, day_correlation(): jnp.einsum('fakb,kft->abt', cross, lag_grid, preferred_element_type=jnp.f...  28.3 us
    reduce_scatter x4, waiting for transfers between devices, body(): lax.psum_scatter(lag_sums.astype(jnp.bfloat16), 'day', scatter_dimension=...  22.1 us
    another operation x1, local copies, waits for them, and re-layouts, day_correlation(): jnp.stack([local, jnp.concatenate([-local[:, 1:2], local[:, 0:1]], axis=1...  15.1 us
  transfers between devices with their start and end apart: 5, of which 2 were waited for; matrix products, arithmetic and copies ran while one was open for 45% of the time, Pallas kernels for 0%

commit v1 on v0

v1 whole, which is shorter than its diff:
```python
import functools
import math

import jax
import jax.numpy as jnp
import numpy as np
from jax import lax
from jax.experimental import pallas as pl
from jax.experimental.pallas import tpu as pltpu
from jax.sharding import PartitionSpec as P

STEPS = 4
LAGS = 256
NFFT = 2400
FIRST_BIN = 60
CHUNK = 128


def lag_table(bins):
    freq = FIRST_BIN + np.arange(bins, dtype=np.int64)
    lag = np.arange(LAGS, dtype=np.int64) - LAGS // 2
    angle = (lag[:, None] * freq[None, :] % NFFT).astype(np.float64) * (2.0 * math.pi / NFFT)
    both = np.concatenate([np.cos(angle), -np.sin(angle)], axis=1)
    return jnp.asarray(both.astype(np.float32)).astype(jnp.bfloat16)


def correlate_kernel(valid_ref, mine_ref, other_ref, own_mine_ref, own_other_ref, table_ref, out_ref,
                     scale_own, scale_loc, turned, rows, side_loc, side_own, cross, packed, lags):
    win, _, ch, bins = mine_ref.shape
    steps, _, _, half, _ = own_mine_ref.shape
    own_ch = steps * half
    terms = 4 * win
    days = ((mine_ref, own_mine_ref), (other_ref, own_other_ref))
    norm = 1.0 / (2.0 * bins)
    cross_scale = 1.0 / math.sqrt(2 * win)

    def energy(x):
        return jnp.sum(x * x, axis=-1, keepdims=True)

    for day, (loc, own) in enumerate(days):
        @pl.loop(0, win)
        def _(w):
            total = energy(loc[w, 0].astype(jnp.float32)) + energy(loc[w, 1].astype(jnp.float32))
            gain = lax.rsqrt(total * norm + 1e-6)
            scale_loc[day * win + w] = jnp.broadcast_to(gain, (ch, 128))
            keep = valid_ref[day, w].astype(jnp.float32)
            for s in range(steps):
                total = energy(own[s, w, 0].astype(jnp.float32)) + energy(own[s, w, 1].astype(jnp.float32))
                gain = lax.rsqrt(total * norm + 1e-6) * keep
                scale_own[day * win + w, s * half:(s + 1) * half] = jnp.broadcast_to(gain, (half, 128))

    @pl.loop(0, bins // CHUNK)
    def _(chunk):
        cols = pl.ds(pl.multiple_of(chunk * CHUNK, CHUNK), CHUNK)
        for day, (loc, own) in enumerate(days):
            @pl.loop(0, win)
            def _(w):
                dw = day * win + w
                for c in range(2):
                    term = dw * 2 + c
                    x = loc[w, c, :, cols].astype(jnp.float32) * scale_loc[dw]
                    rows[pl.ds(pl.multiple_of(term * ch, ch), ch), :] = x
                    o = own[:, w, c, :, cols].astype(jnp.float32).reshape(own_ch, CHUNK) * scale_own[dw]
                    o = jnp.concatenate([o, jnp.zeros((128 - own_ch, CHUNK), jnp.float32)], axis=0).T
                    side_own[0, pl.ds(term, CHUNK, stride=terms), :] = o
                    if c == 0:
                        side_own[1, pl.ds(term + 1, CHUNK, stride=terms), :] = -o
                    else:
                        side_own[1, pl.ds(term - 1, CHUNK, stride=terms), :] = o

        @pl.loop(0, ch, unroll=2)
        def _(b):
            x = rows[pl.ds(b, terms, stride=ch), :]
            x = jnp.concatenate([x, jnp.zeros((128 - terms, CHUNK), jnp.float32)], axis=0).T
            side_loc[pl.ds(b, CHUNK, stride=ch), :] = x

        @pl.loop(0, CHUNK, unroll=8)
        def _(f):
            left = side_loc[pl.ds(pl.multiple_of(f * ch, ch), ch), :][:, :terms].astype(jnp.bfloat16)
            at = pl.ds(pl.multiple_of(f * terms, terms), terms)
            right = jnp.concatenate([side_own[0, at, :], side_own[1, at, :]], axis=1).astype(jnp.bfloat16)
            res = jnp.dot(left, right, preferred_element_type=jnp.float32) * cross_scale
            to = pl.ds(pl.multiple_of(f * ch, ch), ch)
            cross[0, to, :] = res[:, :128]
            cross[1, to, :] = res[:, 128:]

        @pl.loop(0, ch, unroll=2)
        def _(b):
            for k in range(2):
                packed[b, pl.ds(pl.multiple_of(k * bins + chunk * CHUNK, CHUNK), CHUNK), :] = (
                    cross[k, pl.ds(b, CHUNK, stride=ch), :].astype(jnp.bfloat16))

    out_scale = 1.0 / math.sqrt(bins)

    @pl.loop(0, ch // 2)
    def _(pair):
        b = pair * 2
        right = jnp.concatenate([packed[b], packed[b + 1]], axis=1)
        res = jnp.dot(table_ref[...], right, preferred_element_type=jnp.float32) * out_scale
        for i in range(2):
            part = res[:, i * 128:(i + 1) * 128].T[:own_ch]
            for h in range(2):
                lags[h, pl.ds(b + i, own_ch, stride=ch), :] = part[:, h * 128:(h + 1) * 128]

    @pl.loop(0, own_ch)
    def _(i):
        at = pl.ds(pl.multiple_of(i * ch, ch), ch)
        for h in range(2):
            out_ref[i, :, h * 128:(h + 1) * 128] = lags[h, at, :].astype(jnp.bfloat16)


def correlate(valid, mine, other, own_mine, own_other):
    win, _, ch, bins = mine.shape
    steps, _, _, half, _ = own_mine.shape
    own_ch, terms = steps * half, 4 * win
    f32 = jnp.float32
    vmem = pl.BlockSpec(memory_space=pltpu.VMEM)
    out = pl.pallas_call(
        correlate_kernel,
        out_shape=jax.ShapeDtypeStruct((own_ch, ch, LAGS), jnp.bfloat16),
        in_specs=[pl.BlockSpec(memory_space=pltpu.SMEM)] + [vmem] * 5,
        out_specs=vmem,
        scratch_shapes=[
            pltpu.VMEM((2 * win, own_ch, 128), f32),
            pltpu.VMEM((2 * win, ch, 128), f32),
            pltpu.VMEM((8, 128), f32),
            pltpu.VMEM((terms * ch, CHUNK), f32),
            pltpu.VMEM((CHUNK * ch, 128), f32),
            pltpu.VMEM((2, CHUNK * terms, 128), f32),
            pltpu.VMEM((2, CHUNK * ch, 128), f32),
            pltpu.VMEM((ch, 2 * bins, 128), jnp.bfloat16),
            pltpu.VMEM((2, own_ch * ch, 128), f32),
        ],
        compiler_params=pltpu.CompilerParams(vmem_limit_bytes=60 * 1024 * 1024),
        cost_estimate=pl.CostEstimate(flops=4 * 10**9, bytes_accessed=12 * 10**6, transcendentals=0),
    )(valid, mine, other, own_mine, own_other, lag_table(bins))
    return out.reshape(steps, half, ch, LAGS)


def body(spectra, window_valid, owner_order):
    day = lax.axis_index("day")
    me = lax.axis_index("sta")
    mine = spectra[0]
    half = mine.shape[2] // 2
    other = lax.ppermute(mine, "day", [(0, 1), (1, 0)])
    valid = jnp.where(day == 0, window_valid, window_valid[::-1])
    is_owner = (owner_order == me)[:, None, None, None, None]

    def owners(block):
        part = lax.dynamic_slice_in_dim(block, day * half, half, 2)
        return jnp.where(is_owner, part[None], jnp.zeros_like(part[None]))

    own_mine = lax.psum(owners(mine), "sta")
    own_other = lax.psum(owners(other), "sta")
    return correlate(valid, mine, other, own_mine, own_other)


def solution(mesh):
    return jax.shard_map(
        body,
        mesh=mesh,
        in_specs=(P("day", None, None, "sta", None), P(), P()),
        out_specs=P(None, "day", "sta", None),
        check_vma=False,
    )
```

time: 423 us -> 270 us (0.64)
  local copies, waits for them, and re-layouts: 153 us -> 1.96 us
  matrix products: 93.9 us -> 0 us
  Pallas kernels: 0 us -> 82.8 us
  waiting for transfers between devices: 139 us -> 165 us
  other arithmetic: 18.7 us -> 4.37 us
    dot_general x4 -> x0, local copies, waits for them, and re-layouts: 101 us -> none  [day_correlation(): jnp.einsum('wcaf,wckbf->fakb', masked, turned, preferred_element_type=jnp...]
    dot_general x8 -> x0, matrix products: 93.9 us -> none  [the longest x4 65.6 us: day_correlation(): jnp.einsum('wcaf,wckbf->fakb', masked, turned, preferred_element_type=jnp...]
    pallas_call x0 -> x1, Pallas kernels: none -> 82.8 us  [correlate(): pl.pallas_call(correlate_kernel, out_shape=jax.ShapeDtypeStruct((own_ch,...]
    mul x4 -> x0, local copies, waits for them, and re-layouts: 34.2 us -> none  [day_correlation(): masked = owner * day_valid.astype(jnp.bfloat16)[:, None, None, None]]
    ppermute x0 -> x1, waiting for transfers between devices: none -> 30.6 us  [body(): other = lax.ppermute(mine, 'day', [(0, 1), (1, 0)])]
    reduce_scatter x4 -> x0, waiting for transfers between devices: 22.1 us -> none  [body(): lax.psum_scatter(lag_sums.astype(jnp.bfloat16), 'day', scatter_dimension=...]
    psum x1, waiting for transfers between devices: 117 us -> 134 us  [body(): own_mine = lax.psum(owners(mine), 'sta')]
    another operation x1 -> x0, local copies, waits for them, and re-layouts: 15.1 us -> none  [day_correlation(): jnp.stack([local, jnp.concatenate([-local[:, 1:2], local[:, 0:1]], axis=1...]
  transfers between devices with their start and end apart: 5 -> 2, of which waited for: 2 -> 2; matrix products, arithmetic and copies ran while one was open for 45% -> 1% of each run, Pallas kernels for 0% -> 0%
where the time goes in v1:
time: 270 us
  waiting for transfers between devices  165 us (61%)
  Pallas kernels  82.8 us (31%)
  between operations  13.4 us (5%)
  other arithmetic  4.37 us (2%)
  starting transfers between devices  2.94 us (1%)
    psum x1, waiting for transfers between devices, body(): own_mine = lax.psum(owners(mine), 'sta')  134 us
    pallas_call x1, Pallas kernels, correlate(): pl.pallas_call(correlate_kernel, out_shape=jax.ShapeDtypeStruct((own_ch,...  82.8 us
    ppermute x1, waiting for transfers between devices, body(): other = lax.ppermute(mine, 'day', [(0, 1), (1, 0)])  30.6 us
  transfers between devices with their start and end apart: 2, of which 2 were waited for; matrix products, arithmetic and copies ran while one was open for 1% of the time, Pallas kernels for 0%

profile of v1, /device:TPU:0, one launch (start us, length us, event | category | flops | bytes accessed | tf_op | source)
XLA Modules:
  0.0 270.1 jit_solution(11832373266762761512)
XLA Ops:
  6.5 0.0 all-reduce.3.cloned.1.call-start
  6.5 2.9 %collective-permute-start = (bf16[12,2,48,640]{3,2,1,0:T(8,128)(2,1)}, bf16[12,2,48,640]{3,2,1,0:T(8,128)(2,1)S(1)}, u32[]{:S(2)}, u32[]{:S(2)}) collective-permute-start(bf16[12,2,48,640]{3,2,1,0:T(8,128)(2,1)} %bitcast.4), channel_id=1, source_target_pairs={{0,1},{1,0},{2,3},{3,2},{4,5},{5,4},{6,7},{7,6},{8,9},{9,8},{10,11... | collective-permute-start | bytes 4423688 | tf_op jit(solution)/shard_map/ppermute | solution.py:145
  9.5 1.2 dynamic-slice_bitcast_fusion
  10.7 0.7 broadcast_compare_fusion
  11.4 30.6 %collective-permute-done.other_ref = bf16[12,2,48,640]{3,2,1,0:T(8,128)(2,1)S(1)} collective-permute-done((bf16[12,2,48,640]{3,2,1,0:T(8,128)(2,1)}, bf16[12,2,48,640]{3,2,1,0:T(8,128)(2,1)S(1)}, u32[]{:S(2)}, u32[]{:S(2)}) %collective-permute-start) | collective-permute-done | bytes 1474592 | tf_op jit(solution)/shard_map/ppermute | solution.py:145
  42.0 0.0 copy-start
  42.0 0.1 constant_dynamic-slice_fusion
  42.0 3.1 %broadcast_select_fusion = (bf16[4,12,2,24,640]{4,3,2,1,0:T(8,128)(2,1)}, bf16[4,12,2,24,640]{4,3,2,1,0:T(8,128)(2,1)}) fusion(pred[4]{0:T(512)(128)(4,1)S(1)} %broadcast_compare_fusion, bf16[12,2,24,640]{3,2,1,0:T(8,128)(2,1)S(1)} %constant_dynamic-slice_fusion, bf16[12,2,24,640]{3,2,1,0:T(8,128)(2,1)S(1)} %dynamic-slice_bitcast_fusion), kind=kLoop, calls=%fused_computation | loop fusion | flops 2949120 | bytes 7372804 | tf_op jit(solution)/shard_map/jit(_where)/select_n | solution.py:151
  45.2 0.0 copy-done
  45.2 0.0 copy-start.1
  45.2 0.0 all-reduce.3.cloned.1.call-update
  45.2 0.6 copy-done.1
  45.9 0.6 broadcast_select_fusion.2.valid_ref
  46.5 134.0 %all-reduce.3.cloned.1.call-done = (bf16[4,12,2,24,640]{4,3,2,1,0:T(8,128)(2,1)}, bf16[4,12,2,24,640]{4,3,2,1,0:T(8,128)(2,1)}) async-done(((bf16[4,12,2,24,640]{4,3,2,1,0:T(8,128)(2,1)}, bf16[4,12,2,24,640]{4,3,2,1,0:T(8,128)(2,1)}), (bf16[4,12,2,24,640]{4,3,2,1,0:T(8,128)(2,1)}, bf16[4,12,2,24,640]{4,3,2,1,0:T(8,128)(2,1)})) %all-reduce.3.cloned.1.call-update) | async-done | bytes 5898256 | tf_op jit(solution)/shard_map/psum | solution.py:153
  180.5 82.8 %shard_map.46 = bf16[96,48,256]{2,1,0:T(8,128)(2,1)} custom-call(s32[2,12]{1,0:T(2,128)} %broadcast_select_fusion.2.valid_ref, bf16[12,2,48,640]{3,2,1,0:T(8,128)(2,1)} %bitcast.5, bf16[12,2,48,640]{3,2,1,0:T(8,128)(2,1)} %copy-done, bf16[4,12,2,24,640]{4,3,2,1,0:T(8,128)(2,1)} %get-tuple-element.5.own_mine_ref, ...), custom_call_target="tpu_custom_call" | custom-call | flops 4000000000 | bytes 12000000 | tf_op jit(solution)/shard_map/pallas_call | solution.py:118
  (1 shorter events, 0.0 us)
Async XLA Ops:
  6.5 174.0 %all-reduce.3.cloned.1.call-start = ((), (), s32[]{:S(2)}) async-start(), calls=%async_computation | async-start | bytes 11796480 | tf_op jit(solution)/shard_map/psum | solution.py:153
  6.5 35.4 %collective-permute-start = (bf16[12,2,48,640]{3,2,1,0:T(8,128)(2,1)}, bf16[12,2,48,640]{3,2,1,0:T(8,128)(2,1)S(1)}, u32[]{:S(2)}, u32[]{:S(2)}) collective-permute-start(bf16[12,2,48,640]{3,2,1,0:T(8,128)(2,1)} %bitcast.4), channel_id=1, source_target_pairs={{0,1},{1,0},{2,3},{3,2},{4,5},{5,4},{6,7},{7,6},{8,9},{9,8},{10,11... | collective-permute-start | bytes 4423688 | tf_op jit(solution)/shard_map/ppermute | solution.py:145
  42.0 3.2 %copy-start = (bf16[12,2,48,640]{3,2,1,0:T(8,128)(2,1)}, bf16[12,2,48,640]{3,2,1,0:T(8,128)(2,1)S(1)}, u32[]{:S(2)}) copy-start(bf16[12,2,48,640]{3,2,1,0:T(8,128)(2,1)S(1)} %collective-permute-done.other_ref) | copy-start | bytes 4423684
  45.2 0.7 copy-start.1
Sparse Core Ops, SparseCore 0:
  45.3 135.1 all-reduce.2

commit v2 on v1

--- a/solution.py
+++ b/solution.py
@@ -137,22 +137,222 @@
     return out.reshape(steps, half, ch, LAGS)
 
 
+PIECES = 4
+MESH = pl.DeviceIdType.MESH
+
+
+def spread_kernel(chips, gate_ref, keep_ref, give_ref, own_ref, keep_in, give_in,
+                  core_out, core_in, pair_out, pair_in, total, up_in, up_out, down_in, down_out,
+                  day_s, day_r, core_s, core_r, pair_s, pair_r, up_s, up_r, down_s, down_r,
+                  near_s, near_r, far_s, far_r, last_s, last_r):
+    day, me = lax.axis_index("day"), lax.axis_index("sta")
+    core, row, line = lax.rem(me, 2), lax.rem(me // 2, 2), me // 4
+    lines = chips // 2
+    core_dev = {"sta": me + 1 - 2 * core}
+    pair_dev = {"sta": me + 2 - 4 * row}
+    day_dev = {"day": 1 - day}
+    up_dev = {"sta": lax.rem(me + 4, 2 * chips)}
+    down_dev = {"sta": lax.rem(me - 4 + 2 * chips, 2 * chips)}
+    has_up, has_down = line < lines - 1, line > 0
+    late = (line >= lines // 2).astype(jnp.int32)
+    count = 2 * PIECES
+    mine, across = 2 * row + core, 2 * (1 - row) + core
+    mine_core, across_core = 2 * row + 1 - core, 2 * (1 - row) + 1 - core
+
+    def copy(src, dst, send, recv, dev):
+        return pltpu.make_async_remote_copy(
+            src_ref=src, dst_ref=dst, send_sem=send, recv_sem=recv, device_id=dev, device_id_type=MESH)
+
+    def give_copy(k):
+        return copy(give_ref.at[k], keep_in.at[k], day_s.at[k], day_r.at[k], day_dev)
+
+    def keep_copy():
+        return copy(keep_ref, give_in, day_s.at[PIECES], day_r.at[PIECES], day_dev)
+
+    def core_copy(k):
+        return copy(core_out.at[k], core_in.at[k], core_s.at[k], core_r.at[k], core_dev)
+
+    def pair_copy(k):
+        return copy(pair_out.at[k], pair_in.at[k], pair_s.at[k], pair_r.at[k], pair_dev)
+
+    def up_copy(k):
+        return copy(up_out.at[k], up_in.at[k], up_s.at[k], up_r.at[k], up_dev)
+
+    def down_copy(k):
+        return copy(down_out.at[k], down_in.at[k], down_s.at[k], down_r.at[k], down_dev)
+
+    def near_copy(k, slot):
+        return copy(own_ref.at[slot, k], own_ref.at[slot, k], near_s.at[k], near_r.at[k], core_dev)
+
+    def far_copy(k, slot):
+        return copy(own_ref.at[slot, k], own_ref.at[slot, k], far_s.at[k], far_r.at[k], pair_dev)
+
+    def last_copy(k, slot):
+        return copy(own_ref.at[slot, k], own_ref.at[slot, k], last_s.at[k], last_r.at[k], core_dev)
+
+    barrier = pltpu.get_barrier_semaphore()
+    for dev in (core_dev, pair_dev, day_dev):
+        pl.semaphore_signal(barrier, inc=1, device_id=dev, device_id_type=MESH)
+
+    @pl.when(has_up)
+    def _():
+        pl.semaphore_signal(barrier, inc=1, device_id=up_dev, device_id_type=MESH)
+
+    @pl.when(has_down)
+    def _():
+        pl.semaphore_signal(barrier, inc=1, device_id=down_dev, device_id_type=MESH)
+
+    pl.semaphore_wait(barrier, 3 + has_up.astype(jnp.int32) + has_down.astype(jnp.int32))
+
+    for k in range(PIECES):
+        give_copy(k).start()
+    keep_copy().start()
+
+    @pl.when(jnp.logical_not(has_up))
+    def _():
+        down_in[...] = jnp.zeros_like(down_in)
+
+    @pl.when(jnp.logical_not(has_down))
+    def _():
+        up_in[...] = jnp.zeros_like(up_in)
+
+    def gated(block, slot):
+        return (block.astype(jnp.float32) * gate_ref[slot]).astype(jnp.bfloat16)
+
+    for first, source in ((0, keep_ref), (PIECES, keep_in)):
+        @pl.loop(0, PIECES)
+        def _(k):
+            if first:
+                give_copy(k).wait_recv()
+            for j in range(2):
+                core_out[first + k, j] = gated(source[k], 2 * j + 1 - core)
+            core_copy(first + k).start()
+
+        @pl.loop(0, PIECES)
+        def _(k):
+            core_copy(first + k).wait_recv()
+            pair_out[first + k] = gated(source[k], across) + core_in[first + k, 1 - row]
+            pair_copy(first + k).start()
+            total[first + k] = gated(source[k], mine) + core_in[first + k, row]
+
+    @pl.loop(0, count + 6)
+    def _(t):
+        @pl.when(t < count)
+        def _():
+            pair_copy(t).wait_recv()
+            total[t] = total[t] + pair_in[t]
+
+        def up():
+            k = t - 1 - late
+
+            @pl.when(jnp.logical_and(has_up, jnp.logical_and(k >= 0, k < count)))
+            def _():
+                @pl.when(has_down)
+                def _():
+                    up_copy(k).wait_recv()
+                up_out[k] = total[k] + up_in[k]
+                up_copy(k).start()
+
+        def down():
+            k = t - 2 + late
+
+            @pl.when(jnp.logical_and(has_down, jnp.logical_and(k >= 0, k < count)))
+            def _():
+                @pl.when(has_up)
+                def _():
+                    down_copy(k).wait_recv()
+                down_out[k] = total[k] + down_in[k]
+                down_copy(k).start()
+
+        up()
+        down()
+
+        done = t - 4
+
+        @pl.when(jnp.logical_and(done >= 0, done < count))
+        def _():
+            @pl.when(jnp.logical_not(has_up))
+            def _():
+                up_copy(done).wait_recv()
+
+            @pl.when(jnp.logical_not(has_down))
+            def _():
+                down_copy(done).wait_recv()
+            own_ref[mine, done] = total[done] + up_in[done] + down_in[done]
+            far_copy(done, mine).start()
+            near_copy(done, mine).start()
+
+        passed = t - 6
+
+        @pl.when(passed >= 0)
+        def _():
+            far_copy(passed, across).wait_recv()
+            last_copy(passed, across).start()
+
+    for k in range(PIECES):
+        give_copy(k).wait_send()
+    keep_copy().wait()
+
+    @pl.loop(0, count)
+    def _(k):
+        core_copy(k).wait_send()
+        pair_copy(k).wait_send()
+        near_copy(k, mine).wait_send()
+        near_copy(k, mine_core).wait_recv()
+        far_copy(k, mine).wait_send()
+        last_copy(k, across).wait_send()
+        last_copy(k, across_core).wait_recv()
+
+        @pl.when(has_up)
+        def _():
+            up_copy(k).wait_send()
+
+        @pl.when(has_down)
+        def _():
+            down_copy(k).wait_send()
+
+
+def spread(gate, keep, give, stations):
+    win, _, half, bins = keep.shape
+    piece = (win // PIECES, 2, half, bins)
+    count = 2 * PIECES
+    bf16 = jnp.bfloat16
+    vmem = pl.BlockSpec(memory_space=pltpu.VMEM)
+    dma = pltpu.SemaphoreType.DMA
+    own, keep_in, give_in = pl.pallas_call(
+        functools.partial(spread_kernel, stations // 2),
+        out_shape=[
+            jax.ShapeDtypeStruct((STEPS, count) + piece, bf16),
+            jax.ShapeDtypeStruct((PIECES,) + piece, bf16),
+            jax.ShapeDtypeStruct((PIECES,) + piece, bf16),
+        ],
+        in_specs=[pl.BlockSpec(memory_space=pltpu.SMEM), vmem, vmem],
+        out_specs=[vmem] * 3,
+        scratch_shapes=[pltpu.VMEM((count, 2) + piece, bf16)] * 2
+        + [pltpu.VMEM((count,) + piece, bf16)] * 7
+        + [dma((PIECES + 1,))] * 2 + [dma((count,))] * 14,
+        compiler_params=pltpu.CompilerParams(
+            collective_id=0, has_side_effects=True, vmem_limit_bytes=56 * 1024 * 1024),
+    )(gate, keep.reshape((PIECES,) + piece), give.reshape((PIECES,) + piece))
+    shape = (win, 2, half, bins)
+    own = own.reshape((STEPS, 2) + shape)
+    return own, keep_in.reshape(shape), give_in.reshape(shape)
+
+
 def body(spectra, window_valid, owner_order):
     day = lax.axis_index("day")
     me = lax.axis_index("sta")
     mine = spectra[0]
     half = mine.shape[2] // 2
-    other = lax.ppermute(mine, "day", [(0, 1), (1, 0)])
-    valid = jnp.where(day == 0, window_valid, window_valid[::-1])
-    is_owner = (owner_order == me)[:, None, None, None, None]
-
-    def owners(block):
-        part = lax.dynamic_slice_in_dim(block, day * half, half, 2)
-        return jnp.where(is_owner, part[None], jnp.zeros_like(part[None]))
-
-    own_mine = lax.psum(owners(mine), "sta")
-    own_other = lax.psum(owners(other), "sta")
-    return correlate(valid, mine, other, own_mine, own_other)
+    low, high = mine[:, :, :half], mine[:, :, half:]
+    first = day == 0
+    gate = (owner_order == me).astype(jnp.float32)
+    own, keep_in, give_in = spread(
+        gate, jnp.where(first, low, high), jnp.where(first, high, low), lax.axis_size("sta"))
+    other = jnp.concatenate(
+        [jnp.where(first, keep_in, give_in), jnp.where(first, give_in, keep_in)], axis=2)
+    valid = jnp.where(first, window_valid, window_valid[::-1])
+    return correlate(valid, mine, other, own[:, 0], own[:, 1])
 
 
 def solution(mesh):

time: 270 us -> 177 us (0.66)
  waiting for transfers between devices: 165 us -> 0 us
  Pallas kernels: 82.8 us -> 166 us
  between operations: 13.4 us -> 0.03 us
  starting transfers between devices: 2.94 us -> 0 us
    psum x1 -> x0, waiting for transfers between devices: 134 us -> none  [body(): own_mine = lax.psum(owners(mine), 'sta')]
    pallas_call x0 -> x1, Pallas kernels: none -> 83.1 us  [spread(): pl.pallas_call(functools.partial(spread_kernel, stations // 2), out_shape...]
    ppermute x1 -> x0, waiting for transfers between devices: 30.6 us -> none  [body(): other = lax.ppermute(mine, 'day', [(0, 1), (1, 0)])]
    squeeze x0 -> x1, local copies, waits for them, and re-layouts: none -> 3.04 us  [body(): return correlate(valid, mine, other, own[:, 0], own[:, 1])]
    ppermute x1 -> x0, starting transfers between devices: 2.94 us -> none  [body(): other = lax.ppermute(mine, 'day', [(0, 1), (1, 0)])]
  transfers between devices with their start and end apart: 2 -> 0, of which waited for: 2 -> 0; matrix products, arithmetic and copies ran while one was open for 1% -> 0% of each run, Pallas kernels for 0% -> 0%
where the time goes in v2:
time: 177 us; the launch traced here: 176 us
  Pallas kernels  166 us (94%)
  other arithmetic  6.6 us (4%)
  local copies, waits for them, and re-layouts  3.81 us (2%)
    pallas_call x1, Pallas kernels, spread(): pl.pallas_call(functools.partial(spread_kernel, stations // 2), out_shape...  83.1 us
    pallas_call x1, Pallas kernels, correlate(): pl.pallas_call(correlate_kernel, out_shape=jax.ShapeDtypeStruct((own_ch,...  82.8 us

profile of v2, /device:TPU:0, one launch (start us, length us, event | category | flops | bytes accessed | tf_op | source)
XLA Modules:
  0.0 176.3 jit_solution(527797942527261821)
XLA Ops:
  0.0 0.0 copy-start.2
  0.0 2.6 %broadcast_select_fusion = (bf16[12,2,24,640]{3,2,1,0:T(8,128)(2,1)}, bf16[12,2,24,640]{3,2,1,0:T(8,128)(2,1)}) fusion(pred[]{:T(512)S(6)} %eq.9, bf16[12,2,48,640]{3,2,1,0:T(8,128)(2,1)} %bitcast.20), kind=kLoop, calls=%fused_computation.3 | loop fusion | flops 737280 | bytes 2949121 | tf_op jit(solution)/shard_map/jit(_where)/select_n | solution.py:351
  2.6 0.0 copy-done.2
  2.6 0.5 compare_convert_fusion.gate_ref
  3.1 83.1 %shard_map.46 = (bf16[4,8,3,2,24,640]{5,4,3,2,1,0:T(8,128)(2,1)}, bf16[4,3,2,24,640]{4,3,2,1,0:T(8,128)(2,1)}, bf16[4,3,2,24,640]{4,3,2,1,0:T(8,128)(2,1)}) custom-call(f32[4]{0:T(128)} %compare_convert_fusion.gate_ref, bf16[4,3,2,24,640]{4,3,2,1,0:T(8,128)(2,1)} %bitcast.17, bf16[4,3,2,24,640]{4,3,2,1,0:T(8,128)(2,1)} %bitcast.16), custom_call_target="tpu_custom_call" | custom-call | tf_op jit(solution)/shard_map/pallas_call | solution.py:322
  86.3 0.0 copy-start
  86.3 1.6 broadcast_select_fusion.3
  87.9 1.3 pad_maximum_fusion.other_ref
  89.2 0.7 copy-done
  89.9 0.0 copy-start.1
  89.9 3.0 %slice_bitcast_fusion = (bf16[4,12,2,24,640]{4,3,2,1,0:T(8,128)(2,1)}, bf16[4,12,2,24,640]{4,3,2,1,0:T(8,128)(2,1)}) fusion(bf16[4,2,12,2,24,640]{5,4,3,2,1,0:T(8,128)(2,1)S(1)} %bitcast.15), kind=kLoop, calls=%fused_computation | loop fusion | bytes 11796480 | tf_op jit(solution)/shard_map/squeeze | solution.py:355
  93.0 0.0 copy-done.1
  93.0 0.6 broadcast_select_fusion.4.valid_ref
  93.5 82.8 %shard_map.47 = bf16[96,48,256]{2,1,0:T(8,128)(2,1)} custom-call(s32[2,12]{1,0:T(2,128)} %broadcast_select_fusion.4.valid_ref, bf16[12,2,48,640]{3,2,1,0:T(8,128)(2,1)} %bitcast.21, bf16[12,2,48,640]{3,2,1,0:T(8,128)(2,1)} %pad_maximum_fusion.other_ref, bf16[4,12,2,24,640]{4,3,2,1,0:T(8,128)(2,1)} %get-tuple-element.12.own_mine_ref, ...), custom_call_target="tpu_custom_call" | custom-call | flops 4000000000 | bytes 12000000 | tf_op jit(solution)/shard_map/pallas_call | solution.py:118
  (1 shorter events, 0.0 us)
Async XLA Ops:
  0.0 2.6 %copy-start.2 = (s32[4]{0:T(128)S(1)}, s32[4]{0:T(128)}, u32[]{:S(2)}) copy-start(s32[4]{0:T(128)} %param.6) | copy-start | bytes 52
  86.3 3.6 %copy-start = (bf16[4,8,3,2,24,640]{5,4,3,2,1,0:T(8,128)(2,1)S(1)}, bf16[4,8,3,2,24,640]{5,4,3,2,1,0:T(8,128)(2,1)}, u32[]{:S(2)}) copy-start(bf16[4,8,3,2,24,640]{5,4,3,2,1,0:T(8,128)(2,1)} %get-tuple-element.10) | copy-start | bytes 17694724
  89.9 3.0 %copy-start.1 = (s32[2,12]{1,0:T(2,128)S(1)}, s32[2,12]{1,0:T(2,128)}, u32[]{:S(2)}) copy-start(s32[2,12]{1,0:T(2,128)} %param.5) | copy-start | bytes 292

commit v3 on v2

--- a/solution.py
+++ b/solution.py
@@ -14,6 +14,7 @@
 NFFT = 2400
 FIRST_BIN = 60
 CHUNK = 128
+PAD = 1
 
 
 def lag_table(bins):
@@ -25,11 +26,12 @@
 
 
 def correlate_kernel(valid_ref, mine_ref, other_ref, own_mine_ref, own_other_ref, table_ref, out_ref,
-                     scale_own, scale_loc, turned, rows, side_loc, side_own, cross, packed, lags):
+                     scale_own, scale_loc, rows, side_loc, side_own, cross, packed, lags):
     win, _, ch, bins = mine_ref.shape
     steps, _, _, half, _ = own_mine_ref.shape
     own_ch = steps * half
     terms = 4 * win
+    pitch_ch, pitch_terms = ch + PAD, terms + PAD
     days = ((mine_ref, own_mine_ref), (other_ref, own_other_ref))
     norm = 1.0 / (2.0 * bins)
     cross_scale = 1.0 / math.sqrt(2 * win)
@@ -38,7 +40,7 @@
         return jnp.sum(x * x, axis=-1, keepdims=True)
 
     for day, (loc, own) in enumerate(days):
-        @pl.loop(0, win)
+        @pl.loop(0, win, unroll=2)
         def _(w):
             total = energy(loc[w, 0].astype(jnp.float32)) + energy(loc[w, 1].astype(jnp.float32))
             gain = lax.rsqrt(total * norm + 1e-6)
@@ -53,46 +55,46 @@
     def _(chunk):
         cols = pl.ds(pl.multiple_of(chunk * CHUNK, CHUNK), CHUNK)
         for day, (loc, own) in enumerate(days):
-            @pl.loop(0, win)
+            @pl.loop(0, win, unroll=4)
             def _(w):
                 dw = day * win + w
                 for c in range(2):
                     term = dw * 2 + c
                     x = loc[w, c, :, cols].astype(jnp.float32) * scale_loc[dw]
-                    rows[pl.ds(pl.multiple_of(term * ch, ch), ch), :] = x
+                    rows[pl.ds(term * pitch_ch, ch), :] = x
                     o = own[:, w, c, :, cols].astype(jnp.float32).reshape(own_ch, CHUNK) * scale_own[dw]
                     o = jnp.concatenate([o, jnp.zeros((128 - own_ch, CHUNK), jnp.float32)], axis=0).T
-                    side_own[0, pl.ds(term, CHUNK, stride=terms), :] = o
+                    side_own[0, pl.ds(term, CHUNK, stride=pitch_terms), :] = o
                     if c == 0:
-                        side_own[1, pl.ds(term + 1, CHUNK, stride=terms), :] = -o
+                        side_own[1, pl.ds(term + 1, CHUNK, stride=pitch_terms), :] = -o
                     else:
-                        side_own[1, pl.ds(term - 1, CHUNK, stride=terms), :] = o
-
-        @pl.loop(0, ch, unroll=2)
+                        side_own[1, pl.ds(term - 1, CHUNK, stride=pitch_terms), :] = o
+
+        @pl.loop(0, ch, unroll=8)
         def _(b):
-            x = rows[pl.ds(b, terms, stride=ch), :]
+            x = rows[pl.ds(b, terms, stride=pitch_ch), :]
             x = jnp.concatenate([x, jnp.zeros((128 - terms, CHUNK), jnp.float32)], axis=0).T
-            side_loc[pl.ds(b, CHUNK, stride=ch), :] = x
-
-        @pl.loop(0, CHUNK, unroll=8)
+            side_loc[pl.ds(b, CHUNK, stride=pitch_ch), :] = x
+
+        @pl.loop(0, CHUNK, unroll=32)
         def _(f):
-            left = side_loc[pl.ds(pl.multiple_of(f * ch, ch), ch), :][:, :terms].astype(jnp.bfloat16)
-            at = pl.ds(pl.multiple_of(f * terms, terms), terms)
+            left = side_loc[pl.ds(f * pitch_ch, ch), :][:, :terms].astype(jnp.bfloat16)
+            at = pl.ds(f * pitch_terms, terms)
             right = jnp.concatenate([side_own[0, at, :], side_own[1, at, :]], axis=1).astype(jnp.bfloat16)
             res = jnp.dot(left, right, preferred_element_type=jnp.float32) * cross_scale
-            to = pl.ds(pl.multiple_of(f * ch, ch), ch)
+            to = pl.ds(f * pitch_ch, ch)
             cross[0, to, :] = res[:, :128]
             cross[1, to, :] = res[:, 128:]
 
-        @pl.loop(0, ch, unroll=2)
+        @pl.loop(0, ch, unroll=8)
         def _(b):
             for k in range(2):
                 packed[b, pl.ds(pl.multiple_of(k * bins + chunk * CHUNK, CHUNK), CHUNK), :] = (
-                    cross[k, pl.ds(b, CHUNK, stride=ch), :].astype(jnp.bfloat16))
+                    cross[k, pl.ds(b, CHUNK, stride=pitch_ch), :].astype(jnp.bfloat16))
 
     out_scale = 1.0 / math.sqrt(bins)
 
-    @pl.loop(0, ch // 2)
+    @pl.loop(0, ch // 2, unroll=4)
     def _(pair):
         b = pair * 2
         right = jnp.concatenate([packed[b], packed[b + 1]], axis=1)
@@ -100,11 +102,11 @@
         for i in range(2):
             part = res[:, i * 128:(i + 1) * 128].T[:own_ch]
             for h in range(2):
-                lags[h, pl.ds(b + i, own_ch, stride=ch), :] = part[:, h * 128:(h + 1) * 128]
-
-    @pl.loop(0, own_ch)
+                lags[h, pl.ds(b + i, own_ch, stride=pitch_ch), :] = part[:, h * 128:(h + 1) * 128]
+
+    @pl.loop(0, own_ch, unroll=4)
     def _(i):
-        at = pl.ds(pl.multiple_of(i * ch, ch), ch)
+        at = pl.ds(i * pitch_ch, ch)
         for h in range(2):
             out_ref[i, :, h * 128:(h + 1) * 128] = lags[h, at, :].astype(jnp.bfloat16)
 
@@ -123,13 +125,12 @@
         scratch_shapes=[
             pltpu.VMEM((2 * win, own_ch, 128), f32),
             pltpu.VMEM((2 * win, ch, 128), f32),
-            pltpu.VMEM((8, 128), f32),
-            pltpu.VMEM((terms * ch, CHUNK), f32),
-            pltpu.VMEM((CHUNK * ch, 128), f32),
-            pltpu.VMEM((2, CHUNK * terms, 128), f32),
-            pltpu.VMEM((2, CHUNK * ch, 128), f32),
+            pltpu.VMEM(((terms + 1) * (ch + PAD), CHUNK), f32),
+            pltpu.VMEM(((CHUNK + 1) * (ch + PAD), 128), f32),
+            pltpu.VMEM((2, (CHUNK + 1) * (terms + PAD), 128), f32),
+            pltpu.VMEM((2, (CHUNK + 1) * (ch + PAD), 128), f32),
             pltpu.VMEM((ch, 2 * bins, 128), jnp.bfloat16),
-            pltpu.VMEM((2, own_ch * ch, 128), f32),
+            pltpu.VMEM((2, (own_ch + 1) * (ch + PAD), 128), f32),
         ],
         compiler_params=pltpu.CompilerParams(vmem_limit_bytes=60 * 1024 * 1024),
         cost_estimate=pl.CostEstimate(flops=4 * 10**9, bytes_accessed=12 * 10**6, transcendentals=0),

time: 177 us -> 131 us (0.74)
  Pallas kernels: 166 us -> 120 us
    pallas_call x1, Pallas kernels: 82.8 us -> 36.5 us  [correlate(): pl.pallas_call(correlate_kernel, out_shape=jax.ShapeDtypeStruct((own_ch,...]
where the time goes in v3:
time: 131 us; the launch traced here: 130 us
  Pallas kernels  120 us (92%)
  other arithmetic  6.6 us (5%)
  local copies, waits for them, and re-layouts  3.81 us (3%)
    pallas_call x1, Pallas kernels, spread(): pl.pallas_call(functools.partial(spread_kernel, stations // 2), out_shape...  83.1 us
    pallas_call x1, Pallas kernels, correlate(): pl.pallas_call(correlate_kernel, out_shape=jax.ShapeDtypeStruct((own_ch,...  36.5 us
    squeeze x1, local copies, waits for them, and re-layouts, body(): return correlate(valid, mine, other, own[:, 0], own[:, 1])  3.04 us

profile of v3, /device:TPU:0, one launch (start us, length us, event | category | flops | bytes accessed | tf_op | source)
XLA Modules:
  0.0 130.1 jit_solution(12858236903696285511)
XLA Ops:
  0.0 0.0 copy-start.2
  0.0 2.6 %broadcast_select_fusion = (bf16[12,2,24,640]{3,2,1,0:T(8,128)(2,1)}, bf16[12,2,24,640]{3,2,1,0:T(8,128)(2,1)}) fusion(pred[]{:T(512)S(6)} %eq.9, bf16[12,2,48,640]{3,2,1,0:T(8,128)(2,1)} %bitcast.20), kind=kLoop, calls=%fused_computation.3 | loop fusion | flops 737280 | bytes 2949121 | tf_op jit(solution)/shard_map/jit(_where)/select_n | solution.py:352
  2.6 0.0 copy-done.2
  2.6 0.5 compare_convert_fusion.gate_ref
  3.1 83.1 %shard_map.46 = (bf16[4,8,3,2,24,640]{5,4,3,2,1,0:T(8,128)(2,1)}, bf16[4,3,2,24,640]{4,3,2,1,0:T(8,128)(2,1)}, bf16[4,3,2,24,640]{4,3,2,1,0:T(8,128)(2,1)}) custom-call(f32[4]{0:T(128)} %compare_convert_fusion.gate_ref, bf16[4,3,2,24,640]{4,3,2,1,0:T(8,128)(2,1)} %bitcast.17, bf16[4,3,2,24,640]{4,3,2,1,0:T(8,128)(2,1)} %bitcast.16), custom_call_target="tpu_custom_call" | custom-call | tf_op jit(solution)/shard_map/pallas_call | solution.py:323
  86.3 0.0 copy-start
  86.3 1.6 %broadcast_select_fusion.3 = (bf16[4,3,2,24,640]{4,3,2,1,0:T(8,128)(2,1)S(1)}, bf16[4,3,2,24,640]{4,3,2,1,0:T(8,128)(2,1)S(1)}) fusion(bf16[4,3,2,24,640]{4,3,2,1,0:T(8,128)(2,1)} %get-tuple-element.8, bf16[4,3,2,24,640]{4,3,2,1,0:T(8,128)(2,1)} %get-tuple-element.9, pred[]{:T(512)S(6)} %eq.9), kind=kLoop, calls=%fused_computation.6 | loop fusion | flops 737280 | bytes 2949121 | tf_op jit(solution)/shard_map/jit(_where)/select_n | solution.py:354
  87.9 1.3 pad_maximum_fusion.other_ref
  89.2 0.7 copy-done
  89.9 0.0 copy-start.1
  89.9 3.0 %slice_bitcast_fusion = (bf16[4,12,2,24,640]{4,3,2,1,0:T(8,128)(2,1)}, bf16[4,12,2,24,640]{4,3,2,1,0:T(8,128)(2,1)}) fusion(bf16[4,2,12,2,24,640]{5,4,3,2,1,0:T(8,128)(2,1)S(1)} %bitcast.15), kind=kLoop, calls=%fused_computation | loop fusion | bytes 11796480 | tf_op jit(solution)/shard_map/squeeze | solution.py:356
  93.0 0.0 copy-done.1
  93.0 0.6 broadcast_select_fusion.4.valid_ref
  93.5 36.5 %shard_map.47 = bf16[96,48,256]{2,1,0:T(8,128)(2,1)} custom-call(s32[2,12]{1,0:T(2,128)} %broadcast_select_fusion.4.valid_ref, bf16[12,2,48,640]{3,2,1,0:T(8,128)(2,1)} %bitcast.21, bf16[12,2,48,640]{3,2,1,0:T(8,128)(2,1)} %pad_maximum_fusion.other_ref, bf16[4,12,2,24,640]{4,3,2,1,0:T(8,128)(2,1)} %get-tuple-element.12.own_mine_ref, ...), custom_call_target="tpu_custom_call" | custom-call | flops 4000000000 | bytes 12000000 | tf_op jit(solution)/shard_map/pallas_call | solution.py:120
  (1 shorter events, 0.0 us)
Async XLA Ops:
  0.0 2.6 %copy-start.2 = (s32[4]{0:T(128)S(1)}, s32[4]{0:T(128)}, u32[]{:S(2)}) copy-start(s32[4]{0:T(128)} %param.6) | copy-start | bytes 52
  86.3 3.6 %copy-start = (bf16[4,8,3,2,24,640]{5,4,3,2,1,0:T(8,128)(2,1)S(1)}, bf16[4,8,3,2,24,640]{5,4,3,2,1,0:T(8,128)(2,1)}, u32[]{:S(2)}) copy-start(bf16[4,8,3,2,24,640]{5,4,3,2,1,0:T(8,128)(2,1)} %get-tuple-element.10) | copy-start | bytes 17694724
  89.9 3.0 %copy-start.1 = (s32[2,12]{1,0:T(2,128)S(1)}, s32[2,12]{1,0:T(2,128)}, u32[]{:S(2)}) copy-start(s32[2,12]{1,0:T(2,128)} %param.5) | copy-start | bytes 292

commit v4 on v3

--- a/solution.py
+++ b/solution.py
@@ -25,21 +25,21 @@
     return jnp.asarray(both.astype(np.float32)).astype(jnp.bfloat16)
 
 
-def correlate_kernel(valid_ref, mine_ref, other_ref, own_mine_ref, own_other_ref, table_ref, out_ref,
+def correlate_kernel(valid_ref, mine_ref, other_ref, own_ref, table_ref, out_ref,
                      scale_own, scale_loc, rows, side_loc, side_own, cross, packed, lags):
     win, _, ch, bins = mine_ref.shape
-    steps, _, _, half, _ = own_mine_ref.shape
+    steps, _, _, _, half, _ = own_ref.shape
     own_ch = steps * half
     terms = 4 * win
     pitch_ch, pitch_terms = ch + PAD, terms + PAD
-    days = ((mine_ref, own_mine_ref), (other_ref, own_other_ref))
+    days = (mine_ref, other_ref)
     norm = 1.0 / (2.0 * bins)
     cross_scale = 1.0 / math.sqrt(2 * win)
 
     def energy(x):
         return jnp.sum(x * x, axis=-1, keepdims=True)
 
-    for day, (loc, own) in enumerate(days):
+    for day, loc in enumerate(days):
         @pl.loop(0, win, unroll=2)
         def _(w):
             total = energy(loc[w, 0].astype(jnp.float32)) + energy(loc[w, 1].astype(jnp.float32))
@@ -47,14 +47,14 @@
             scale_loc[day * win + w] = jnp.broadcast_to(gain, (ch, 128))
             keep = valid_ref[day, w].astype(jnp.float32)
             for s in range(steps):
-                total = energy(own[s, w, 0].astype(jnp.float32)) + energy(own[s, w, 1].astype(jnp.float32))
+                total = energy(own_ref[s, day, w, 0].astype(jnp.float32)) + energy(own_ref[s, day, w, 1].astype(jnp.float32))
                 gain = lax.rsqrt(total * norm + 1e-6) * keep
                 scale_own[day * win + w, s * half:(s + 1) * half] = jnp.broadcast_to(gain, (half, 128))
 
     @pl.loop(0, bins // CHUNK)
     def _(chunk):
         cols = pl.ds(pl.multiple_of(chunk * CHUNK, CHUNK), CHUNK)
-        for day, (loc, own) in enumerate(days):
+        for day, loc in enumerate(days):
             @pl.loop(0, win, unroll=4)
             def _(w):
                 dw = day * win + w
@@ -62,7 +62,7 @@
                     term = dw * 2 + c
                     x = loc[w, c, :, cols].astype(jnp.float32) * scale_loc[dw]
                     rows[pl.ds(term * pitch_ch, ch), :] = x
-                    o = own[:, w, c, :, cols].astype(jnp.float32).reshape(own_ch, CHUNK) * scale_own[dw]
+                    o = own_ref[:, day, w, c, :, cols].astype(jnp.float32).reshape(own_ch, CHUNK) * scale_own[dw]
                     o = jnp.concatenate([o, jnp.zeros((128 - own_ch, CHUNK), jnp.float32)], axis=0).T
                     side_own[0, pl.ds(term, CHUNK, stride=pitch_terms), :] = o
                     if c == 0:
@@ -111,16 +111,16 @@
             out_ref[i, :, h * 128:(h + 1) * 128] = lags[h, at, :].astype(jnp.bfloat16)
 
 
-def correlate(valid, mine, other, own_mine, own_other):
+def correlate(valid, mine, other, own):
     win, _, ch, bins = mine.shape
-    steps, _, _, half, _ = own_mine.shape
+    steps, _, _, _, half, _ = own.shape
     own_ch, terms = steps * half, 4 * win
     f32 = jnp.float32
     vmem = pl.BlockSpec(memory_space=pltpu.VMEM)
     out = pl.pallas_call(
         correlate_kernel,
         out_shape=jax.ShapeDtypeStruct((own_ch, ch, LAGS), jnp.bfloat16),
-        in_specs=[pl.BlockSpec(memory_space=pltpu.SMEM)] + [vmem] * 5,
+        in_specs=[pl.BlockSpec(memory_space=pltpu.SMEM)] + [vmem] * 4,
         out_specs=vmem,
         scratch_shapes=[
             pltpu.VMEM((2 * win, own_ch, 128), f32),
@@ -134,7 +134,7 @@
         ],
         compiler_params=pltpu.CompilerParams(vmem_limit_bytes=60 * 1024 * 1024),
         cost_estimate=pl.CostEstimate(flops=4 * 10**9, bytes_accessed=12 * 10**6, transcendentals=0),
-    )(valid, mine, other, own_mine, own_other, lag_table(bins))
+    )(valid, mine, other, own, lag_table(bins))
     return out.reshape(steps, half, ch, LAGS)
 
 
@@ -207,7 +207,6 @@
 
     for k in range(PIECES):
         give_copy(k).start()
-    keep_copy().start()
 
     @pl.when(jnp.logical_not(has_up))
     def _():
@@ -228,6 +227,9 @@
             for j in range(2):
                 core_out[first + k, j] = gated(source[k], 2 * j + 1 - core)
             core_copy(first + k).start()
+
+        if first:
+            keep_copy().start()
 
         @pl.loop(0, PIECES)
         def _(k):
@@ -353,7 +355,7 @@
     other = jnp.concatenate(
         [jnp.where(first, keep_in, give_in), jnp.where(first, give_in, keep_in)], axis=2)
     valid = jnp.where(first, window_valid, window_valid[::-1])
-    return correlate(valid, mine, other, own[:, 0], own[:, 1])
+    return correlate(valid, mine, other, own)
 
 
 def solution(mesh):

time: 131 us -> 128 us (0.977)
  local copies, waits for them, and re-layouts: 3.81 us -> 0.7 us
    squeeze x1 -> x0, local copies, waits for them, and re-layouts: 3.04 us -> none  [body(): return correlate(valid, mine, other, own[:, 0], own[:, 1])]
where the time goes in v4:
time: 128 us; the launch traced here: 127 us
  Pallas kernels  119 us (93%)
  other arithmetic  7.79 us (6%)
    pallas_call x1, Pallas kernels, spread(): pl.pallas_call(functools.partial(spread_kernel, stations // 2), out_shape...  82.4 us
    pallas_call x1, Pallas kernels, correlate(): pl.pallas_call(correlate_kernel, out_shape=jax.ShapeDtypeStruct((own_ch,...  36.5 us
    select_n x1, other arithmetic, body(): jnp.where(first, high, low)  2.6 us

profile of v4, /device:TPU:0, one launch (start us, length us, event | category | flops | bytes accessed | tf_op | source)
XLA Modules:
  0.0 127.5 jit_solution(3795917441149581029)
XLA Ops:
  0.0 1.2 compare_convert_fusion.gate_ref
  1.2 0.7 rev.3
  1.9 1.3 broadcast_select_fusion.4.valid_ref
  3.1 2.6 %broadcast_select_fusion = (bf16[12,2,24,640]{3,2,1,0:T(8,128)(2,1)}, bf16[12,2,24,640]{3,2,1,0:T(8,128)(2,1)}) fusion(pred[]{:T(512)S(6)} %eq.9, bf16[12,2,48,640]{3,2,1,0:T(8,128)(2,1)} %bitcast.11), kind=kLoop, calls=%fused_computation.1 | loop fusion | flops 737280 | bytes 2949121 | tf_op jit(solution)/shard_map/jit(_where)/select_n | solution.py:354
  5.7 82.4 %shard_map.46 = (bf16[4,8,3,2,24,640]{5,4,3,2,1,0:T(8,128)(2,1)}, bf16[4,3,2,24,640]{4,3,2,1,0:T(8,128)(2,1)}, bf16[4,3,2,24,640]{4,3,2,1,0:T(8,128)(2,1)}) custom-call(f32[4]{0:T(128)} %compare_convert_fusion.gate_ref, bf16[4,3,2,24,640]{4,3,2,1,0:T(8,128)(2,1)} %bitcast.8, bf16[4,3,2,24,640]{4,3,2,1,0:T(8,128)(2,1)} %bitcast.7), custom_call_target="tpu_custom_call" | custom-call | tf_op jit(solution)/shard_map/pallas_call | solution.py:325
  88.2 1.5 %broadcast_select_fusion.3 = (bf16[4,3,2,24,640]{4,3,2,1,0:T(8,128)(2,1)S(1)}, bf16[4,3,2,24,640]{4,3,2,1,0:T(8,128)(2,1)S(1)}) fusion(bf16[4,3,2,24,640]{4,3,2,1,0:T(8,128)(2,1)} %get-tuple-element.8, bf16[4,3,2,24,640]{4,3,2,1,0:T(8,128)(2,1)} %get-tuple-element.9, pred[]{:T(512)S(6)} %eq.9), kind=kLoop, calls=%fused_computation.4 | loop fusion | flops 737280 | bytes 2949121 | tf_op jit(solution)/shard_map/jit(_where)/select_n | solution.py:356
  89.7 1.3 %pad_maximum_fusion.other_ref = bf16[12,2,48,640]{3,2,1,0:T(8,128)(2,1)} fusion(bf16[12,2,24,640]{3,2,1,0:T(8,128)(2,1)S(1)} %bitcast.10, bf16[12,2,24,640]{3,2,1,0:T(8,128)(2,1)S(1)} %bitcast.9), kind=kLoop, calls=%fused_computation | loop fusion | flops 2949120 | bytes 2949120 | tf_op jit(solution)/shard_map/concatenate | solution.py:355
  90.9 36.5 %shard_map.47 = bf16[96,48,256]{2,1,0:T(8,128)(2,1)} custom-call(s32[2,12]{1,0:T(2,128)} %broadcast_select_fusion.4.valid_ref, bf16[12,2,48,640]{3,2,1,0:T(8,128)(2,1)} %bitcast.12, bf16[12,2,48,640]{3,2,1,0:T(8,128)(2,1)} %pad_maximum_fusion.other_ref, bf16[4,2,12,2,24,640]{5,4,3,2,1,0:T(8,128)(2,1)} %bitcast.13, bf16[256,1280]{1,0:T(8,128)(2,1)} %constant.14.table_ref), custom_call_target="tpu_custom_call" | custom-call | flops 4000000000 | bytes 12000000 | tf_op jit(solution)/shard_map/pallas_call | solution.py:120

commit v5 on v4

--- a/solution.py
+++ b/solution.py
@@ -55,7 +55,7 @@
     def _(chunk):
         cols = pl.ds(pl.multiple_of(chunk * CHUNK, CHUNK), CHUNK)
         for day, loc in enumerate(days):
-            @pl.loop(0, win, unroll=4)
+            @pl.loop(0, win, unroll=6)
             def _(w):
                 dw = day * win + w
                 for c in range(2):
@@ -70,7 +70,7 @@
                     else:
                         side_own[1, pl.ds(term - 1, CHUNK, stride=pitch_terms), :] = o
 
-        @pl.loop(0, ch, unroll=8)
+        @pl.loop(0, ch, unroll=12)
         def _(b):
             x = rows[pl.ds(b, terms, stride=pitch_ch), :]
             x = jnp.concatenate([x, jnp.zeros((128 - terms, CHUNK), jnp.float32)], axis=0).T
@@ -86,7 +86,7 @@
             cross[0, to, :] = res[:, :128]
             cross[1, to, :] = res[:, 128:]
 
-        @pl.loop(0, ch, unroll=8)
+        @pl.loop(0, ch, unroll=12)
         def _(b):
             for k in range(2):
                 packed[b, pl.ds(pl.multiple_of(k * bins + chunk * CHUNK, CHUNK), CHUNK), :] = (
@@ -94,7 +94,7 @@
 
     out_scale = 1.0 / math.sqrt(bins)
 
-    @pl.loop(0, ch // 2, unroll=4)
+    @pl.loop(0, ch // 2, unroll=6)
     def _(pair):
         b = pair * 2
         right = jnp.concatenate([packed[b], packed[b + 1]], axis=1)
@@ -104,7 +104,7 @@
             for h in range(2):
                 lags[h, pl.ds(b + i, own_ch, stride=pitch_ch), :] = part[:, h * 128:(h + 1) * 128]
 
-    @pl.loop(0, own_ch, unroll=4)
+    @pl.loop(0, own_ch, unroll=8)
     def _(i):
         at = pl.ds(i * pitch_ch, ch)
         for h in range(2):

time: 128 us -> 126 us (0.984)
  Pallas kernels: 119 us -> 117 us
    pallas_call x1, Pallas kernels: 36.5 us -> 34.2 us  [correlate(): pl.pallas_call(correlate_kernel, out_shape=jax.ShapeDtypeStruct((own_ch,...]
where the time goes in v5:
time: 126 us; the launch traced here: 125 us
  Pallas kernels  117 us (93%)
  other arithmetic  7.79 us (6%)
    pallas_call x1, Pallas kernels, spread(): pl.pallas_call(functools.partial(spread_kernel, stations // 2), out_shape...  82.4 us
    pallas_call x1, Pallas kernels, correlate(): pl.pallas_call(correlate_kernel, out_shape=jax.ShapeDtypeStruct((own_ch,...  34.2 us
    select_n x1, other arithmetic, body(): jnp.where(first, high, low)  2.6 us

profile of v5, /device:TPU:0, one launch (start us, length us, event | category | flops | bytes accessed | tf_op | source)
XLA Modules:
  0.0 125.2 jit_solution(11301229792389570548)
XLA Ops:
  0.0 1.2 compare_convert_fusion.gate_ref
  1.2 0.7 rev.3
  1.9 1.3 %broadcast_select_fusion.4.valid_ref = s32[2,12]{1,0:T(2,128)} fusion(s32[2,12]{1,0:T(2,128)} %param.5, s32[2,12]{1,0:T(2,128)S(1)} %rev.3, pred[]{:T(512)S(6)} %eq.9), kind=kLoop, calls=%fused_computation.6 | loop fusion | flops 24 | bytes 289 | tf_op jit(solution)/shard_map/jit(_where)/select_n | solution.py:357
  3.1 2.6 %broadcast_select_fusion = (bf16[12,2,24,640]{3,2,1,0:T(8,128)(2,1)}, bf16[12,2,24,640]{3,2,1,0:T(8,128)(2,1)}) fusion(pred[]{:T(512)S(6)} %eq.9, bf16[12,2,48,640]{3,2,1,0:T(8,128)(2,1)} %bitcast.11), kind=kLoop, calls=%fused_computation.1 | loop fusion | flops 737280 | bytes 2949121 | tf_op jit(solution)/shard_map/jit(_where)/select_n | solution.py:354
  5.7 82.4 %shard_map.46 = (bf16[4,8,3,2,24,640]{5,4,3,2,1,0:T(8,128)(2,1)}, bf16[4,3,2,24,640]{4,3,2,1,0:T(8,128)(2,1)}, bf16[4,3,2,24,640]{4,3,2,1,0:T(8,128)(2,1)}) custom-call(f32[4]{0:T(128)} %compare_convert_fusion.gate_ref, bf16[4,3,2,24,640]{4,3,2,1,0:T(8,128)(2,1)} %bitcast.8, bf16[4,3,2,24,640]{4,3,2,1,0:T(8,128)(2,1)} %bitcast.7), custom_call_target="tpu_custom_call" | custom-call | tf_op jit(solution)/shard_map/pallas_call | solution.py:325
  88.2 1.5 %broadcast_select_fusion.3 = (bf16[4,3,2,24,640]{4,3,2,1,0:T(8,128)(2,1)S(1)}, bf16[4,3,2,24,640]{4,3,2,1,0:T(8,128)(2,1)S(1)}) fusion(bf16[4,3,2,24,640]{4,3,2,1,0:T(8,128)(2,1)} %get-tuple-element.8, bf16[4,3,2,24,640]{4,3,2,1,0:T(8,128)(2,1)} %get-tuple-element.9, pred[]{:T(512)S(6)} %eq.9), kind=kLoop, calls=%fused_computation.4 | loop fusion | flops 737280 | bytes 2949121 | tf_op jit(solution)/shard_map/jit(_where)/select_n | solution.py:356
  89.7 1.3 %pad_maximum_fusion.other_ref = bf16[12,2,48,640]{3,2,1,0:T(8,128)(2,1)} fusion(bf16[12,2,24,640]{3,2,1,0:T(8,128)(2,1)S(1)} %bitcast.10, bf16[12,2,24,640]{3,2,1,0:T(8,128)(2,1)S(1)} %bitcast.9), kind=kLoop, calls=%fused_computation | loop fusion | flops 2949120 | bytes 2949120 | tf_op jit(solution)/shard_map/concatenate | solution.py:355
  90.9 34.2 %shard_map.47 = bf16[96,48,256]{2,1,0:T(8,128)(2,1)} custom-call(s32[2,12]{1,0:T(2,128)} %broadcast_select_fusion.4.valid_ref, bf16[12,2,48,640]{3,2,1,0:T(8,128)(2,1)} %bitcast.12, bf16[12,2,48,640]{3,2,1,0:T(8,128)(2,1)} %pad_maximum_fusion.other_ref, bf16[4,2,12,2,24,640]{5,4,3,2,1,0:T(8,128)(2,1)} %bitcast.13, bf16[256,1280]{1,0:T(8,128)(2,1)} %constant.14.table_ref), custom_call_target="tpu_custom_call" | custom-call | flops 4000000000 | bytes 12000000 | tf_op jit(solution)/shard_map/pallas_call | solution.py:120
